TPU v7x, 512 devices: a whole 4x4x16 slice. The times are simulated.
512 devices in a mesh: term: 32 (over y, x, core), sector: 16 (over z).
Axes of the slice: x: 4, y: 4, z: 16, core: 2. Of those that a mesh axis runs over, the one named last changes fastest.
Arguments:
- wavefunction: bfloat16 [96, 256, 256], P('sector')
- left_operator_blocks: bfloat16 [384, 256, 256], P('term'), may hold values from -0.01953125 to 0.01953125
- right_operator_blocks: bfloat16 [384, 256, 256], P('term'), may hold values from -0.375 to 0.375
- fetch_index: int32 [32, 16, 16], P('term', 'sector'), may hold values from 0 to 5, as said below
- owner_link: int32 [384, 96], P('term', 'sector'), may hold values from 0 to 15, as said below
- lower_roots: bfloat16 [4, 96, 256, 256], P(None, 'sector', 'term')
- level_shift: float32 [4], replicated, may hold values from 0.5 to 2
Outputs:
- sigma: float32 [96, 256, 256], P('sector', 'term')
- correlations: float32 [4], replicated
Inputs may be any that keep to these rules, and one draw needn't show every extreme that they name: `fetch_index`: entry p of every list is a position within the 6 sectors of sector index p. `owner_link`: within the 12 x 6 entries that one device holds, every sector index occurs at least once.
All inputs are finite; a program needn't handle non-finite values.
Results may differ from a plain program's by a relative error of at most 0.0059.
Values may be sent and summed in bfloat16 or wider, within the bound.
A program may use at most 64 MiB of HBM per device.

v0:
```python
import jax
import jax.numpy as jnp
from jax import lax
from jax.sharding import PartitionSpec as P


def per_device(
    wavefunction,
    left_operator_blocks,
    right_operator_blocks,
    fetch_index,
    owner_link,
    lower_roots,
    level_shift,
):
    sec_dev = wavefunction.shape[0]
    block_width = wavefunction.shape[1]
    group_count = fetch_index.shape[2]
    own_requests = fetch_index.reshape(group_count, 1)
    store = lax.all_gather(wavefunction, "sector", axis=0, tiled=True)
    lookup = owner_link * sec_dev + own_requests[:, 0][owner_link]

    def one_sector(column):
        input_sectors = store[column]
        partial_contraction = jnp.einsum(
            "lhm,lmp->lhp", left_operator_blocks, input_sectors, preferred_element_type=jnp.float32
        ).astype(jnp.bfloat16)
        return jnp.einsum(
            "yxz,ysz->xs",
            partial_contraction,
            right_operator_blocks,
            preferred_element_type=jnp.float32,
        )

    partial_value = lax.map(one_sector, jnp.transpose(lookup))
    reduced = lax.psum_scatter(partial_value, "term", scatter_dimension=1, tiled=True)
    row_count = reduced.shape[1]
    row_start = lax.axis_index("term") * row_count
    psi_rows = lax.dynamic_slice_in_dim(wavefunction, row_start, row_count, 1)
    local_correlation = jnp.einsum(
        "ksab,sab->k", lower_roots, psi_rows, preferred_element_type=jnp.float32
    )
    total_cells = lax.axis_size("sector") * sec_dev * block_width * block_width
    correlations = lax.psum(local_correlation, ("term", "sector")) / total_cells
    sigma = reduced + jnp.einsum(
        "k,ksab->sab", level_shift * correlations, lower_roots.astype(jnp.float32)
    )
    return (sigma, correlations)


def solution(mesh):
    return jax.shard_map(
        per_device,
        mesh=mesh,
        in_specs=(
            P("sector", None, None),
            P("term", None, None),
            P("term", None, None),
            P("term", "sector", None),
            P("term", "sector"),
            P(None, "sector", "term", None),
            P(),
        ),
        out_specs=(P("sector", "term", None), P()),
        check_vma=False,
    )
```

profile of v0, /device:TPU:1, one launch (start us, length us, event | category | flops | bytes accessed | tf_op | source)
XLA Modules:
  0.0 328.3 jit_solution(2077307641894323809)
XLA Ops:
  7.2 0.0 copy-start
  7.2 0.0 copy-start.1
  7.2 0.0 all-gather.2.cloned.1.call-start
  7.2 0.7 all-gather.2.cloned.1.call-update
  7.9 0.0 reduce-scatter.2.cloned.1.call-start
  8.0 0.8 copy.17
  8.8 0.7 compare_select_fusion.1
  9.4 0.1 copy.18
  9.5 0.1 reshape.42
  9.6 0.0 copy-done.1
  9.7 0.0 copy-start.2
  9.7 1.2 gather_fusion.1
  10.9 0.1 reshape.41
  11.0 0.1 copy.19
  11.1 152.4 %all-gather.2.cloned.1.call-done = bf16[96,256,256]{2,1,0:T(8,128)(2,1)} async-done(((bf16[6,256,256]{2,1,0:T(8,128)(2,1)}), bf16[96,256,256]{2,1,0:T(8,128)(2,1)}) %all-gather.2.cloned.1.call-update) | async-done | bytes 12582928 | tf_op jit(solution)/shard_map/all_gather | solution.py:20
  163.5 0.0 copy-done.2
  163.5 52.1 %while.10 = (s32[]{:T(128)}, f32[6,256,256]{2,1,0:T(8,128)}, s32[6,12]{1,0:T(8,128)S(1)}, bf16[96,256,256]{2,1,0:T(8,128)(2,1)}, bf16[12,256,256]{2,1,0:T(8,128)...) while((s32[]{:T(128)}, f32[6,256,256]{2,1,0:T(8,128)}, s32[6,12]{1,0:T(8,128)S(1)}, ...), condition=%wide.region_1.2_spmd, body=%wide.region_0.1_spmd.sunk | while | flops 806093888 | bytes 8130845 | solution.py:35
  163.5 5.2 %gather_fusion = bf16[12,256,256]{2,1,0:T(8,128)(2,1)S(1)} fusion(bf16[96,256,256]{2,1,0:T(8,128)(2,1)} %get-tuple-element.119, s32[1024]{0:T(1024)S(1)} %pad_clamp_fusion.3), kind=kCustom, calls=%fused_computation.clone.1 | custom fusion | bytes 3145776 | tf_op jit(solution)/shard_map/while/body/eval_jaxpr/gather | solution.py:24
  168.8 3.4 %fusion.27 = f32[6,256,256]{2,1,0:T(8,128)} fusion(f32[6,256,256]{2,1,0:T(8,128)} %get-tuple-element.110, s32[]{:T(128)S(6)} %copy.38, bf16[12,256,256]{2,1,0:T(8,128)(2,1)} %get-tuple-element.121, bf16[12,256,256]{2,1,0:T(8,128)(2,1)S(1)} %gather_fusion, bf16[12,256,256]{2,1,0:T(8,128)(2,1)S(1)} %get-tuple-element.120), kind=kOutput, calls=%fused_computation.6.clone.1 | convolution fusion | flops 806092800 | bytes 4980740 | tf_op jit(solution)/shard_map/while/body/eval_jaxpr/yxz,ysz->xs/dot_general | solution.py:28
  172.2 5.2 %gather_fusion = bf16[12,256,256]{2,1,0:T(8,128)(2,1)S(1)} fusion(bf16[96,256,256]{2,1,0:T(8,128)(2,1)} %get-tuple-element.119, s32[1024]{0:T(1024)S(1)} %pad_clamp_fusion.3), kind=kCustom, calls=%fused_computation.clone.1 | custom fusion | bytes 3145776 | tf_op jit(solution)/shard_map/while/body/eval_jaxpr/gather | solution.py:24
  177.4 3.5 %fusion.27 = f32[6,256,256]{2,1,0:T(8,128)} fusion(f32[6,256,256]{2,1,0:T(8,128)} %get-tuple-element.110, s32[]{:T(128)S(6)} %copy.38, bf16[12,256,256]{2,1,0:T(8,128)(2,1)} %get-tuple-element.121, bf16[12,256,256]{2,1,0:T(8,128)(2,1)S(1)} %gather_fusion, bf16[12,256,256]{2,1,0:T(8,128)(2,1)S(1)} %get-tuple-element.120), kind=kOutput, calls=%fused_computation.6.clone.1 | convolution fusion | flops 806092800 | bytes 4980740 | tf_op jit(solution)/shard_map/while/body/eval_jaxpr/yxz,ysz->xs/dot_general | solution.py:28
  180.9 5.2 %gather_fusion = bf16[12,256,256]{2,1,0:T(8,128)(2,1)S(1)} fusion(bf16[96,256,256]{2,1,0:T(8,128)(2,1)} %get-tuple-element.119, s32[1024]{0:T(1024)S(1)} %pad_clamp_fusion.3), kind=kCustom, calls=%fused_computation.clone.1 | custom fusion | bytes 3145776 | tf_op jit(solution)/shard_map/while/body/eval_jaxpr/gather | solution.py:24
  186.1 3.4 %fusion.27 = f32[6,256,256]{2,1,0:T(8,128)} fusion(f32[6,256,256]{2,1,0:T(8,128)} %get-tuple-element.110, s32[]{:T(128)S(6)} %copy.38, bf16[12,256,256]{2,1,0:T(8,128)(2,1)} %get-tuple-element.121, bf16[12,256,256]{2,1,0:T(8,128)(2,1)S(1)} %gather_fusion, bf16[12,256,256]{2,1,0:T(8,128)(2,1)S(1)} %get-tuple-element.120), kind=kOutput, calls=%fused_computation.6.clone.1 | convolution fusion | flops 806092800 | bytes 4980740 | tf_op jit(solution)/shard_map/while/body/eval_jaxpr/yxz,ysz->xs/dot_general | solution.py:28
  189.6 5.2 %gather_fusion = bf16[12,256,256]{2,1,0:T(8,128)(2,1)S(1)} fusion(bf16[96,256,256]{2,1,0:T(8,128)(2,1)} %get-tuple-element.119, s32[1024]{0:T(1024)S(1)} %pad_clamp_fusion.3), kind=kCustom, calls=%fused_computation.clone.1 | custom fusion | bytes 3145776 | tf_op jit(solution)/shard_map/while/body/eval_jaxpr/gather | solution.py:24
  194.8 3.4 %fusion.27 = f32[6,256,256]{2,1,0:T(8,128)} fusion(f32[6,256,256]{2,1,0:T(8,128)} %get-tuple-element.110, s32[]{:T(128)S(6)} %copy.38, bf16[12,256,256]{2,1,0:T(8,128)(2,1)} %get-tuple-element.121, bf16[12,256,256]{2,1,0:T(8,128)(2,1)S(1)} %gather_fusion, bf16[12,256,256]{2,1,0:T(8,128)(2,1)S(1)} %get-tuple-element.120), kind=kOutput, calls=%fused_computation.6.clone.1 | convolution fusion | flops 806092800 | bytes 4980740 | tf_op jit(solution)/shard_map/while/body/eval_jaxpr/yxz,ysz->xs/dot_general | solution.py:28
  198.3 5.2 %gather_fusion = bf16[12,256,256]{2,1,0:T(8,128)(2,1)S(1)} fusion(bf16[96,256,256]{2,1,0:T(8,128)(2,1)} %get-tuple-element.119, s32[1024]{0:T(1024)S(1)} %pad_clamp_fusion.3), kind=kCustom, calls=%fused_computation.clone.1 | custom fusion | bytes 3145776 | tf_op jit(solution)/shard_map/while/body/eval_jaxpr/gather | solution.py:24
  203.5 3.4 %fusion.27 = f32[6,256,256]{2,1,0:T(8,128)} fusion(f32[6,256,256]{2,1,0:T(8,128)} %get-tuple-element.110, s32[]{:T(128)S(6)} %copy.38, bf16[12,256,256]{2,1,0:T(8,128)(2,1)} %get-tuple-element.121, bf16[12,256,256]{2,1,0:T(8,128)(2,1)S(1)} %gather_fusion, bf16[12,256,256]{2,1,0:T(8,128)(2,1)S(1)} %get-tuple-element.120), kind=kOutput, calls=%fused_computation.6.clone.1 | convolution fusion | flops 806092800 | bytes 4980740 | tf_op jit(solution)/shard_map/while/body/eval_jaxpr/yxz,ysz->xs/dot_general | solution.py:28
  206.9 5.2 %gather_fusion = bf16[12,256,256]{2,1,0:T(8,128)(2,1)S(1)} fusion(bf16[96,256,256]{2,1,0:T(8,128)(2,1)} %get-tuple-element.119, s32[1024]{0:T(1024)S(1)} %pad_clamp_fusion.3), kind=kCustom, calls=%fused_computation.clone.1 | custom fusion | bytes 3145776 | tf_op jit(solution)/shard_map/while/body/eval_jaxpr/gather | solution.py:24
  212.2 3.4 %fusion.27 = f32[6,256,256]{2,1,0:T(8,128)} fusion(f32[6,256,256]{2,1,0:T(8,128)} %get-tuple-element.110, s32[]{:T(128)S(6)} %copy.38, bf16[12,256,256]{2,1,0:T(8,128)(2,1)} %get-tuple-element.121, bf16[12,256,256]{2,1,0:T(8,128)(2,1)S(1)} %gather_fusion, bf16[12,256,256]{2,1,0:T(8,128)(2,1)S(1)} %get-tuple-element.120), kind=kOutput, calls=%fused_computation.6.clone.1 | convolution fusion | flops 806092800 | bytes 4980740 | tf_op jit(solution)/shard_map/while/body/eval_jaxpr/yxz,ysz->xs/dot_general | solution.py:28
  215.6 0.0 copy-start.3
  215.6 0.0 reduce-scatter.2.cloned.1.call-update
  215.6 0.7 dynamic-slice_bitcast_fusion
  216.4 0.0 copy-done
  216.4 0.3 convolution_bitcast_fusion
  216.6 103.1 %psum.7 = f32[4]{0:T(128)S(1)} all-reduce(f32[4]{0:T(128)S(1)} %convolution_bitcast_fusion), channel_id=1, replica_groups=mesh['term'=32,'sector'=16] {'term','sector'}, use_global_device_ids=true, to_apply=%region_3.4 | all-reduce | flops 4 | bytes 32 | tf_op jit(solution)/shard_map/psum | solution.py:44
  319.8 0.0 copy-done.3
  319.8 0.0 copy-start.4
  319.8 0.2 fusion.9
  320.0 0.0 reduce-scatter.2.cloned.1.call-done
  320.0 1.4 bitcast_add_fusion
  321.4 0.0 copy-done.4
  (16 shorter events, 0.1 us)
Async XLA Ops:
  7.2 209.2 %copy-start = (bf16[4,6,8,256]{3,2,1,0:T(8,128)(2,1)S(1)}, bf16[4,6,8,256]{3,2,1,0:T(8,128)(2,1)}, u32[]{:S(2)}) copy-start(bf16[4,6,8,256]{3,2,1,0:T(8,128)(2,1)} %param.14) | copy-start | bytes 294916
  7.2 2.5 copy-start.1
  7.2 156.3 %all-gather.2.cloned.1.call-start = ((), (), s32[]{:S(2)}) async-start(), calls=%async_computation.1 | async-start | bytes 13369344 | tf_op jit(solution)/shard_map/all_gather | solution.py:20
  7.9 312.1 %reduce-scatter.2.cloned.1.call-start = ((), (), s32[]{:S(2)}) async-start(), calls=%async_computation.2 | async-start | bytes 1622016 | tf_op jit(solution)/shard_map/reduce_scatter | solution.py:36
  9.7 153.9 %copy-start.2 = (bf16[12,256,256]{2,1,0:T(8,128)(2,1)S(1)}, bf16[12,256,256]{2,1,0:T(8,128)(2,1)}, u32[]{:S(2)}) copy-start(bf16[12,256,256]{2,1,0:T(8,128)(2,1)} %param.10) | copy-start | bytes 4718596
  215.6 104.2 %copy-start.3 = (f32[4]{0:T(128)S(1)}, f32[4]{0:T(128)}, u32[]{:S(2)}) copy-start(f32[4]{0:T(128)} %param.15) | copy-start | bytes 52
  319.8 1.6 copy-start.4
Sparse Core Ops, SparseCore 0:
  10.1 153.3 all-gather.1
  215.8 97.6 reduce-scatter.1
where the time goes:
time: 329 us; the launch traced here: 328 us
  waiting for transfers between devices  153 us (47%)
  blocking collectives  103 us (31%)
  local copies, waits for them, and re-layouts  34.5 us (10%)
  matrix products  21 us (6%)
  between operations  14.1 us (4%)
    all_gather x1, waiting for transfers between devices, per_device(): store = lax.all_gather(wavefunction, 'sector', axis=0, tiled=True)  152 us
    psum x1, blocking collectives, per_device(): correlations = lax.psum(local_correlation, ('term', 'sector')) / total_cells  103 us
    gather x6, local copies, waits for them, and re-layouts, one_sector(): input_sectors = store[column]  31.3 us
    dot_general x6, matrix products, one_sector(): jnp.einsum('yxz,ysz->xs', partial_contraction, right_operator_blocks, pre...  20.6 us
  transfers between devices with their start and end apart: 2, of which 1 were waited for; matrix products, arithmetic and copies ran while one was open for 1% of the time, Pallas kernels for 0%

commit v1 on v0

v1 whole, which is shorter than its diff:
```python
import jax
import jax.numpy as jnp
from jax import lax
from jax.experimental import pallas as pl
from jax.experimental.pallas import tpu as pltpu
from jax.sharding import PartitionSpec as P

BF = jnp.bfloat16
F32 = jnp.float32
MESH = pl.DeviceIdType.MESH
NY, NX, NZ = 4, 4, 16
PLANE = 2 * NY * NX
SEC, TERM, B, ROOTS = 6, 12, 256, 4
CELLS = NZ * SEC * B * B
NEAR = 4
SOURCE = {1: 0, 2: 1, 3: 2, 4: 3, 5: 0, 6: 5, 7: 6, 8: 7}
EVENTS = (
    "O0", "F0", "Z1", "P1", "Z5", "Q0", "P5", "Z2", "P2", "C1", "Z6", "P6", "Z3", "P3", "C5",
    "Z7", "P7", "C2", "C6", "Z8", "P8", "Z4", "P4", "C3", "C7", "C8", "C4",
)


def term_of(y, x, c):
    return (y * NX + x) * 2 + c


def kernel(psi_hbm, fetch_v, fetch_s, owner, lb_hbm, rb_hbm, roots_hbm, part_out, corr_out, *scr):
    psi, roots = scr[:2]
    st = (None,) + scr[2:10]
    sb = scr[10:18]
    (blocks, lb, rcat, half, reqv, reqs, corr_buf, corr_mine, part, d2d_s, d2d_r, rs_s, rs_r,
     load_sem, z_send, z_recv, p_send, p_recv, req_send, req_recv, req_local, c_send, c_recv,
     d_send, d_recv, r_send, r_recv) = scr[18:]
    t = lax.axis_index("term")
    z = lax.axis_index("sector")
    y, x, c = t // (2 * NX), (t // 2) % NX, t % 2
    chip = t // 2

    barrier = pltpu.get_barrier_semaphore()
    peers = []
    for dz in range(1, NZ):
        peers.append((t, (z + dz) % NZ))
    for i in range(1, PLANE):
        peers.append(((t + i) % PLANE, z))
    for peer in peers:
        pl.semaphore_signal(barrier, inc=1, device_id=peer, device_id_type=MESH)

    load_psi = pltpu.make_async_copy(psi_hbm, psi, load_sem.at[TERM + 1])
    load_psi.start()
    load_roots = pltpu.make_async_copy(roots_hbm, roots, load_sem.at[TERM + 2])
    load_roots.start()
    load_l = pltpu.make_async_copy(lb_hbm, lb, load_sem.at[TERM])
    load_l.start()
    load_r = []
    for i in range(TERM):
        copy = pltpu.make_async_copy(rb_hbm.at[i], rcat.at[:, pl.ds(i * B, B)], load_sem.at[i])
        copy.start()
        load_r.append(copy)

    reqv[t] = jnp.zeros((1, 128), jnp.int32)
    reqv[t, :, 0:NZ] = fetch_v[...]

    pl.semaphore_wait(barrier, len(peers))

    def remote(src, dst, send, recv, peer):
        return pltpu.make_async_remote_copy(
            src, dst, send, recv, device_id=peer, device_id_type=MESH
        )

    def wait_bytes(ref, sem):
        pltpu.make_async_copy(ref, ref, sem).wait()

    def quarter(k):
        return jnp.where((z + k + c) % 2 == 0, y, x)

    col = pl.multiple_of(c * 128, 128)

    def z_copy(k, d, h, src_k):
        hop = k - src_k
        peer = (t, (z + (hop if d == 0 else NZ - hop)) % NZ)
        sl = pl.ds(h * 3, 3)
        own = quarter(src_k) * 64 if k <= NEAR else chip * 16
        own = pl.ds(pl.multiple_of(own, 16), 64 if k <= NEAR else 16)
        if src_k == 0:
            src = psi.at[sl, own, pl.ds(col, 128)]
        else:
            src = st[src_k].at[d, sl]
        dst = st[k].at[d, sl] if k < 8 else st[k].at[0, sl]
        n = ((k - 1) * 2 + d) * 2 + h
        return remote(src, dst, z_send.at[n], z_recv.at[n], peer)

    def halves(k, d):
        return (0, 1) if k < 8 else (d,)

    def z_start(k, d):
        for h in halves(k, d):
            z_copy(k, d, h, SOURCE[k]).start()

    def z_event(k):
        for h in (0, 1):
            for d in (0, 1):
                if h in halves(k, d):
                    z_copy(k, d, h, SOURCE[k]).wait_recv()
                for later in range(k + 1, 9):
                    if SOURCE[later] == k and h in halves(later, d):
                        z_copy(later, d, h, k).start()

    def dirs(k):
        return 1 if k == 8 else 2

    def select(k, peer, store):
        for d in range(dirs(k)):
            p = (z + (NZ - k if d == 0 else k)) % NZ
            store(d, st[k][d, reqs[peer, 0, p]])

    def p_event(k):
        if k <= NEAR:
            start, size = quarter(k) * 64, 64
        else:
            start, size = chip * 16, 16
        rows = pl.ds(pl.multiple_of(start, 16), size)
        dst = blocks.at[k - 1, 0:dirs(k), c, rows, :]

        def keep(d, piece):
            blocks[k - 1, d, c, rows, :] = piece

        def send(n, peer):
            def stage(d, piece):
                sb[k - 1][n, d] = piece

            select(k, peer, stage)
            remote(sb[k - 1].at[n], dst, p_send.at[k - 1], p_recv.at[k - 1], (peer, z)).start()

        select(k, t, keep)
        if k <= NEAR:
            even = (z + k + c) % 2 == 0
            for n in range(1, 8):
                dq, dc = n // 2, n % 2
                yy = jnp.where(even, (y + dq) % NY, y)
                xx = jnp.where(even, x, (x + dq) % NX)
                send(n - 1, term_of(yy, xx, (c + dc) % 2))
        else:
            @pl.loop(1, PLANE)
            def _(i):
                send(i - 1, lax.rem(t + i, PLANE))

    def p_whole(k):
        return sb[k - 1]

    def first_products(rel, block):
        half[rel] = jnp.dot(lb[...], block, preferred_element_type=F32).astype(BF)

    def c_event(k):
        wait_bytes(p_whole(k), p_recv.at[k - 1])
        for d in range(dirs(k)):
            block = jnp.concatenate([blocks[k - 1, d, 0], blocks[k - 1, d, 1]], axis=1)
            first_products(NZ - k if d == 0 else k, block)

    groups = (
        (t, [((t + i) % PLANE, z) for i in range(1, PLANE)]),
        (z, [(t, (z + i) % NZ) for i in range(1, NZ)]),
    )

    def q_start(g):
        slot, others = groups[g]
        corr_buf[g, slot] = corr_mine[g]
        for peer in others:
            remote(corr_mine.at[g], corr_buf.at[g, slot], c_send.at[g], c_recv.at[g], peer).start()

    def q_event(g):
        n = len(groups[g][1])
        wait_bytes(corr_buf.at[g, pl.ds(0, n)], c_recv.at[g])
        total = corr_buf[g, 0]
        for i in range(1, n + 1):
            total = total + corr_buf[g, i]
        corr_mine[g + 1] = total
        if g + 1 < len(groups):
            q_start(g + 1)

    for i in range(1, PLANE):
        remote(reqv.at[t], reqv.at[t], req_send, req_recv, ((t + i) % PLANE, z)).start()
    load_psi.wait()
    for d in (0, 1):
        for k in range(1, 9):
            if SOURCE[k] == 0:
                z_start(k, d)
    load_roots.wait()
    rows16 = psi[:, pl.ds(pl.multiple_of(chip * 16, 16), 16), :].astype(F32)
    mine = jnp.where(c == 0, rows16[:, :8, :], rows16[:, 8:, :])
    lines = []
    for k in range(ROOTS):
        prod = jnp.sum(roots[k].astype(F32) * mine, axis=0)
        prod = prod[:, :128] + prod[:, 128:]
        lines.append(jnp.sum(prod, axis=0, keepdims=True))
    corr_mine[0] = jnp.concatenate(lines + [jnp.zeros((8 - ROOTS, 128), F32)], axis=0)
    q_start(0)

    def own_event(_):
        load_l.wait()
        first_products(0, psi[fetch_s[0, z]])

    def f_event(_):
        wait_bytes(reqv.at[pl.ds(0, PLANE - 1)], req_recv)
        to_scalars = pltpu.make_async_copy(reqv, reqs, req_local)
        to_scalars.start()
        to_scalars.wait()

    for event in EVENTS:
        arg = int(event[1:])
        {
            "Z": z_event, "P": p_event, "C": c_event, "Q": q_event, "F": f_event, "O": own_event,
        }[event[0]](arg)

    for copy in load_r:
        copy.wait()

    def sector_sum(s):
        def place(i):
            return (owner[s, i] + NZ - z) % NZ

        total = None
        for g in range(0, TERM, 4):
            lhs = jnp.concatenate([half[place(i), pl.ds(i * B, B)] for i in range(g, g + 4)], axis=1)
            prod = lax.dot_general(
                lhs, rcat[:, g * B:(g + 4) * B], (((1,), (1,)), ((), ())), preferred_element_type=F32
            )
            total = prod if total is None else total + prod
        return total.reshape(16, 2, 8, B)

    sibling = (term_of(y, x, 1 - c), z)

    def d2d(u):
        return remote(d2d_s.at[u], d2d_r.at[u], d_send.at[u], d_recv.at[u], sibling)

    def rs_start(u):
        d2d(u).wait_recv()
        total = part[u] + d2d_r[u].astype(F32)
        part[u] = total
        rs_s[u] = total.astype(BF)
        for i in range(1, 16):
            ch = (chip + i) % 16
            remote(rs_s.at[u, ch], rs_r.at[u, chip], r_send.at[u], r_recv.at[u], (ch * 2 + c, z)).start()

    for u in range(3):
        for e in range(2):
            both = sector_sum(2 * u + e)
            keep = jnp.where(c == 0, both[:, 0], both[:, 1])
            give = jnp.where(c == 0, both[:, 1], both[:, 0])
            part[u, :, e * 8:(e + 1) * 8, :] = keep
            d2d_keep = give
            if e == 0:
                part[3, :, 0:8, :] = d2d_keep
            else:
                part[3, :, 8:16, :] = d2d_keep
        d2d_s[u] = part[3].astype(BF)
        d2d(u).start()
        if u > 0:
            rs_start(u - 1)
    rs_start(2)

    q_event(1)
    corr_out[...] = corr_mine[len(groups)]

    for k in range(1, 9):
        for d in (0, 1):
            for h in halves(k, d):
                z_copy(k, d, h, SOURCE[k]).wait_send()
        wait_bytes(p_whole(k), p_send.at[k - 1])
    wait_bytes(reqv.at[pl.ds(0, PLANE - 1)], req_send)
    for g in range(len(groups)):
        wait_bytes(corr_buf.at[g, pl.ds(0, len(groups[g][1]))], c_send.at[g])

    for u in range(3):
        rs_r[u, chip] = jnp.zeros((16, B), BF)
        wait_bytes(rs_s.at[u, pl.ds(0, 15)], r_recv.at[u])
        total = part[u, chip]
        for i in range(16):
            total = total + rs_r[u, i].astype(F32)
        part_out[u] = total
    for u in range(3):
        d2d(u).wait_send()
        wait_bytes(rs_s.at[u, pl.ds(0, 15)], r_send.at[u])


def finish(part, corr_rows, shift, roots, sig, corr_out):
    corr = jnp.sum(corr_rows[...], axis=1, keepdims=True) * (1.0 / CELLS)
    for s in range(SEC):
        out = part[s // 2, s % 2 * 8:s % 2 * 8 + 8]
        for k in range(ROOTS):
            out = out + (corr[k:k + 1] * shift[k]) * roots[k, s].astype(F32)
        sig[s] = out
    for k in range(ROOTS):
        corr_out[k] = jnp.sum(corr[k:k + 1])


def per_device(psi, lb, rb, fetch, owner, roots, shift):
    fetch = fetch.reshape(1, NZ)
    vm = pl.BlockSpec(memory_space=pltpu.VMEM)
    sm = pl.BlockSpec(memory_space=pltpu.SMEM)
    hbm = pl.BlockSpec(memory_space=pl.ANY)
    dma = pltpu.SemaphoreType.DMA
    scratch = [pltpu.VMEM((SEC, B, B), BF), pltpu.VMEM((ROOTS, SEC, 8, B), BF)]
    sizes = [(64 if k <= NEAR else 16, 1 if k == 8 else 2, 7 if k <= NEAR else PLANE - 1) for k in range(1, 9)]
    scratch += [pltpu.VMEM((dirs, SEC, rows, 128), BF) for rows, dirs, _ in sizes]
    scratch += [pltpu.VMEM((count, dirs, rows, 128), BF) for rows, dirs, count in sizes]
    scratch += [
        pltpu.VMEM((8, 2, 2, B, 128), BF),
        pltpu.VMEM((TERM * B, B), BF),
        pltpu.VMEM((B, TERM * B), BF),
        pltpu.VMEM((NZ, TERM * B, B), BF),
        pltpu.VMEM((PLANE, 1, 128), jnp.int32),
        pltpu.SMEM((PLANE, 1, 128), jnp.int32),
        pltpu.VMEM((2, PLANE, 8, 128), F32),
        pltpu.VMEM((3, 8, 128), F32),
        pltpu.VMEM((4, 16, 16, B), F32),
        pltpu.VMEM((3, 16, 16, B), BF),
        pltpu.VMEM((3, 16, 16, B), BF),
        pltpu.VMEM((3, 16, 16, B), BF),
        pltpu.VMEM((3, 16, 16, B), BF),
        dma((TERM + 3,)), dma((32,)), dma((32,)), dma((8,)), dma((8,)),
        dma, dma, dma, dma((2,)), dma((2,)), dma((3,)), dma((3,)), dma((3,)), dma((3,)),
    ]
    part, corr_rows = pl.pallas_call(
        kernel,
        out_shape=(
            jax.ShapeDtypeStruct((3, 16, B), F32),
            jax.ShapeDtypeStruct((8, 128), F32),
        ),
        in_specs=[hbm, vm, sm, sm, hbm, hbm, hbm],
        out_specs=(vm, vm),
        scratch_shapes=scratch,
        compiler_params=pltpu.CompilerParams(
            collective_id=0, has_side_effects=True, vmem_limit_bytes=56 << 20
        ),
    )(psi, fetch, fetch, owner.T, lb.reshape(TERM * B, B), rb, roots)
    return pl.pallas_call(
        finish,
        out_shape=(
            jax.ShapeDtypeStruct((SEC, 8, B), F32),
            jax.ShapeDtypeStruct((ROOTS,), F32),
        ),
        in_specs=[vm, vm, sm, vm],
        out_specs=(vm, sm),
    )(part, corr_rows, shift, roots)


def solution(mesh):
    return jax.shard_map(
        per_device,
        mesh=mesh,
        in_specs=(
            P("sector", None, None),
            P("term", None, None),
            P("term", None, None),
            P("term", "sector", None),
            P("term", "sector"),
            P(None, "sector", "term", None),
            P(),
        ),
        out_specs=(P("sector", "term", None), P()),
        check_vma=False,
    )
```

time: 329 us -> 60.2 us (0.18)
  waiting for transfers between devices: 153 us -> 0 us
  blocking collectives: 103 us -> 0 us
  Pallas kernels: 0 us -> 59.4 us
  local copies, waits for them, and re-layouts: 34.5 us -> 0 us
  matrix products: 21 us -> 0 us
  between operations: 14.1 us -> 0.64 us
    all_gather x1 -> x0, waiting for transfers between devices: 152 us -> none  [per_device(): store = lax.all_gather(wavefunction, 'sector', axis=0, tiled=True)]
    psum x1 -> x0, blocking collectives: 103 us -> none  [per_device(): correlations = lax.psum(local_correlation, ('term', 'sector')) / total_cells]
    pallas_call x0 -> x2, Pallas kernels: none -> 59.4 us  [the longest x1 57.7 us: per_device(): pl.pallas_call(kernel, out_shape=(jax.ShapeDtypeStruct((3, 16, B), F32),...]
    gather x8 -> x0, local copies, waits for them, and re-layouts: 32.6 us -> none  [the longest x6 31.3 us: one_sector(): input_sectors = store[column]]
    dot_general x8 -> x0, matrix products: 21 us -> none  [the longest x6 20.6 us: one_sector(): jnp.einsum('yxz,ysz->xs', partial_contraction, right_operator_blocks, pre...]
  transfers between devices with their start and end apart: 2 -> 0, of which waited for: 1 -> 0; matrix products, arithmetic and copies ran while one was open for 1% -> 0% of each run, Pallas kernels for 0% -> 0%
where the time goes in v1:
time: 60.2 us; the launch traced here: 60 us
  Pallas kernels  59.4 us (99%)
  between operations  0.64 us (1%)
    pallas_call x1, Pallas kernels, per_device(): pl.pallas_call(kernel, out_shape=(jax.ShapeDtypeStruct((3, 16, B), F32),...  57.7 us
    pallas_call x1, Pallas kernels, per_device(): pl.pallas_call(finish, out_shape=(jax.ShapeDtypeStruct((SEC, 8, B), F32),...  1.66 us

profile of v1, /device:TPU:1, one launch (start us, length us, event | category | flops | bytes accessed | tf_op | source)
XLA Modules:
  0.0 60.0 jit_solution(18300008495427178377)
XLA Ops:
  0.6 57.7 %shard_map.86 = (f32[3,16,256]{2,1,0:T(8,128)}, f32[8,128]{1,0:T(8,128)}) custom-call(bf16[6,256,256]{2,1,0:T(8,128)(2,1)} %psi_hbm.1, s32[1,16]{1,0:T(1,128)} %bitcast.5, s32[1,16]{1,0:T(1,128)} %bitcast.6, s32[6,12]{1,0:T(8,128)} %bitcast.4, bf16[3072,256]{1,0:T(8,128)(2,1)} %bitcast.3, bf16[12,256,256]{2,1,0:T(8,128)(2,1)} %rb_hbm.1, ...), custom_call_target="tpu_custom_call" | custom-call | tf_op jit(solution)/shard_map/pallas_call | solution.py:323
  58.4 1.7 %shard_map.87 = (f32[6,8,256]{2,1,0:T(8,128)}, f32[4]{0:T(128)}) custom-call(f32[3,16,256]{2,1,0:T(8,128)} %get-tuple-element.4.part, f32[8,128]{1,0:T(8,128)} %get-tuple-element.5.corr_rows, f32[4]{0:T(128)} %shift.1, bf16[4,6,8,256]{3,2,1,0:T(8,128)(2,1)} %roots.1), custom_call_target="tpu_custom_call" | custom-call | tf_op jit(solution)/shard_map/pallas_call | solution.py:336

commit v2 on v1

--- a/solution.py
+++ b/solution.py
@@ -15,8 +15,8 @@
 NEAR = 4
 SOURCE = {1: 0, 2: 1, 3: 2, 4: 3, 5: 0, 6: 5, 7: 6, 8: 7}
 EVENTS = (
-    "O0", "F0", "Z1", "P1", "Z5", "Q0", "P5", "Z2", "P2", "C1", "Z6", "P6", "Z3", "P3", "C5",
-    "Z7", "P7", "C2", "C6", "Z8", "P8", "Z4", "P4", "C3", "C7", "C8", "C4",
+    "O0", "F0", "Z1", "P1", "Z5", "P5", "Z2", "P2", "C1", "Z6", "P6", "Z3", "P3", "C5", "Z7",
+    "P7", "C2", "C6", "Z8", "P8", "Z4", "P4", "C3", "C7", "Q0", "C8", "C4",
 )
 
 
@@ -28,8 +28,8 @@
     psi, roots = scr[:2]
     st = (None,) + scr[2:10]
     sb = scr[10:18]
-    (blocks, lb, rcat, half, reqv, reqs, corr_buf, corr_mine, part, d2d_s, d2d_r, rs_s, rs_r,
-     load_sem, z_send, z_recv, p_send, p_recv, req_send, req_recv, req_local, c_send, c_recv,
+    (blocks, lb, rcat, half, reqv, reqs, corr_buf, corr_z, part, d2d_s, d2d_r, rs_s, rs_r,
+     load_sem, z_send, z_recv, p_send, p_recv, req_send, req_recv, req_local, c_send, c_recv, qz_send, qz_recv,
      d_send, d_recv, r_send, r_recv) = scr[18:]
     t = lax.axis_index("term")
     z = lax.axis_index("sector")
@@ -38,7 +38,8 @@
 
     barrier = pltpu.get_barrier_semaphore()
     peers = []
-    for dz in range(1, NZ):
+    hops = {k - source for k, source in SOURCE.items()}
+    for dz in sorted(hops | {NZ - h for h in hops}):
         peers.append((t, (z + dz) % NZ))
     for i in range(1, PLANE):
         peers.append(((t + i) % PLANE, z))
@@ -89,6 +90,16 @@
         n = ((k - 1) * 2 + d) * 2 + h
         return remote(src, dst, z_send.at[n], z_recv.at[n], peer)
 
+    def dirs(k):
+        return 1 if k == 8 else 2
+
+    def q_copy(k, d, src_k):
+        hop = k - src_k
+        plane = (z + (NZ - src_k if d == 0 else src_k)) % NZ
+        src = corr_z.at[plane]
+        peer = (t, (z + (hop if d == 0 else NZ - hop)) % NZ)
+        return remote(src, src, qz_send.at[k - 1, d], qz_recv.at[k - 1, d], peer)
+
     def halves(k, d):
         return (0, 1) if k < 8 else (d,)
 
@@ -104,9 +115,11 @@
                 for later in range(k + 1, 9):
                     if SOURCE[later] == k and h in halves(later, d):
                         z_copy(later, d, h, k).start()
-
-    def dirs(k):
-        return 1 if k == 8 else 2
+        for d in range(dirs(k)):
+            q_copy(k, d, SOURCE[k]).wait_recv()
+            for later in range(k + 1, 9):
+                if SOURCE[later] == k and d < dirs(later):
+                    q_copy(later, d, k).start()
 
     def select(k, peer, store):
         for d in range(dirs(k)):
@@ -156,26 +169,22 @@
             block = jnp.concatenate([blocks[k - 1, d, 0], blocks[k - 1, d, 1]], axis=1)
             first_products(NZ - k if d == 0 else k, block)
 
-    groups = (
-        (t, [((t + i) % PLANE, z) for i in range(1, PLANE)]),
-        (z, [(t, (z + i) % NZ) for i in range(1, NZ)]),
-    )
-
-    def q_start(g):
-        slot, others = groups[g]
-        corr_buf[g, slot] = corr_mine[g]
-        for peer in others:
-            remote(corr_mine.at[g], corr_buf.at[g, slot], c_send.at[g], c_recv.at[g], peer).start()
-
-    def q_event(g):
-        n = len(groups[g][1])
-        wait_bytes(corr_buf.at[g, pl.ds(0, n)], c_recv.at[g])
-        total = corr_buf[g, 0]
-        for i in range(1, n + 1):
-            total = total + corr_buf[g, i]
-        corr_mine[g + 1] = total
-        if g + 1 < len(groups):
-            q_start(g + 1)
+    def q_event(_):
+        total = corr_z[0]
+        for i in range(1, NZ):
+            total = total + corr_z[i]
+        corr_buf[t] = total
+
+        @pl.loop(1, PLANE)
+        def _(i):
+            remote(corr_buf.at[t], corr_buf.at[t], c_send, c_recv, (lax.rem(t + i, PLANE), z)).start()
+
+    def q_total():
+        wait_bytes(corr_buf.at[pl.ds(0, PLANE - 1)], c_recv)
+        total = corr_buf[0]
+        for i in range(1, PLANE):
+            total = total + corr_buf[i]
+        return total
 
     for i in range(1, PLANE):
         remote(reqv.at[t], reqv.at[t], req_send, req_recv, ((t + i) % PLANE, z)).start()
@@ -192,8 +201,11 @@
         prod = jnp.sum(roots[k].astype(F32) * mine, axis=0)
         prod = prod[:, :128] + prod[:, 128:]
         lines.append(jnp.sum(prod, axis=0, keepdims=True))
-    corr_mine[0] = jnp.concatenate(lines + [jnp.zeros((8 - ROOTS, 128), F32)], axis=0)
-    q_start(0)
+    corr_z[z] = jnp.concatenate(lines + [jnp.zeros((8 - ROOTS, 128), F32)], axis=0)
+    for k in range(1, 9):
+        for d in range(dirs(k)):
+            if SOURCE[k] == 0:
+                q_copy(k, d, 0).start()
 
     def own_event(_):
         load_l.wait()
@@ -258,17 +270,17 @@
             rs_start(u - 1)
     rs_start(2)
 
-    q_event(1)
-    corr_out[...] = corr_mine[len(groups)]
+    corr_out[...] = q_total()
 
     for k in range(1, 9):
         for d in (0, 1):
             for h in halves(k, d):
                 z_copy(k, d, h, SOURCE[k]).wait_send()
+            if d < dirs(k):
+                q_copy(k, d, SOURCE[k]).wait_send()
         wait_bytes(p_whole(k), p_send.at[k - 1])
     wait_bytes(reqv.at[pl.ds(0, PLANE - 1)], req_send)
-    for g in range(len(groups)):
-        wait_bytes(corr_buf.at[g, pl.ds(0, len(groups[g][1]))], c_send.at[g])
+    wait_bytes(corr_buf.at[pl.ds(0, PLANE - 1)], c_send)
 
     for u in range(3):
         rs_r[u, chip] = jnp.zeros((16, B), BF)
@@ -310,15 +322,15 @@
         pltpu.VMEM((NZ, TERM * B, B), BF),
         pltpu.VMEM((PLANE, 1, 128), jnp.int32),
         pltpu.SMEM((PLANE, 1, 128), jnp.int32),
-        pltpu.VMEM((2, PLANE, 8, 128), F32),
-        pltpu.VMEM((3, 8, 128), F32),
+        pltpu.VMEM((PLANE, 8, 128), F32),
+        pltpu.VMEM((NZ, 8, 128), F32),
         pltpu.VMEM((4, 16, 16, B), F32),
         pltpu.VMEM((3, 16, 16, B), BF),
         pltpu.VMEM((3, 16, 16, B), BF),
         pltpu.VMEM((3, 16, 16, B), BF),
         pltpu.VMEM((3, 16, 16, B), BF),
         dma((TERM + 3,)), dma((32,)), dma((32,)), dma((8,)), dma((8,)),
-        dma, dma, dma, dma((2,)), dma((2,)), dma((3,)), dma((3,)), dma((3,)), dma((3,)),
+        dma, dma, dma, dma, dma, dma((8, 2)), dma((8, 2)), dma((3,)), dma((3,)), dma((3,)), dma((3,)),
     ]
     part, corr_rows = pl.pallas_call(
         kernel,

time: 60.2 us -> 59.1 us (0.982)
  Pallas kernels: 59.4 us -> 58.3 us
    pallas_call x1, Pallas kernels: 57.7 us -> 56.6 us  [per_device(): pl.pallas_call(kernel, out_shape=(jax.ShapeDtypeStruct((3, 16, B), F32),...]
where the time goes in v2:
time: 59.1 us; the launch traced here: 58.9 us
  Pallas kernels  58.3 us (99%)
  between operations  0.64 us (1%)
    pallas_call x1, Pallas kernels, per_device(): pl.pallas_call(kernel, out_shape=(jax.ShapeDtypeStruct((3, 16, B), F32),...  56.6 us
    pallas_call x1, Pallas kernels, per_device(): pl.pallas_call(finish, out_shape=(jax.ShapeDtypeStruct((SEC, 8, B), F32),...  1.66 us

profile of v2, /device:TPU:1, one launch (start us, length us, event | category | flops | bytes accessed | tf_op | source)
XLA Modules:
  0.0 58.9 jit_solution(16977187728337847722)
XLA Ops:
  0.6 56.6 %shard_map.86 = (f32[3,16,256]{2,1,0:T(8,128)}, f32[8,128]{1,0:T(8,128)}) custom-call(bf16[6,256,256]{2,1,0:T(8,128)(2,1)} %psi_hbm.1, s32[1,16]{1,0:T(1,128)} %bitcast.5, s32[1,16]{1,0:T(1,128)} %bitcast.6, s32[6,12]{1,0:T(8,128)} %bitcast.4, bf16[3072,256]{1,0:T(8,128)(2,1)} %bitcast.3, bf16[12,256,256]{2,1,0:T(8,128)(2,1)} %rb_hbm.1, ...), custom_call_target="tpu_custom_call" | custom-call | tf_op jit(solution)/shard_map/pallas_call | solution.py:335
  57.2 1.7 %shard_map.87 = (f32[6,8,256]{2,1,0:T(8,128)}, f32[4]{0:T(128)}) custom-call(f32[3,16,256]{2,1,0:T(8,128)} %get-tuple-element.4.part, f32[8,128]{1,0:T(8,128)} %get-tuple-element.5.corr_rows, f32[4]{0:T(128)} %shift.1, bf16[4,6,8,256]{3,2,1,0:T(8,128)(2,1)} %roots.1), custom_call_target="tpu_custom_call" | custom-call | tf_op jit(solution)/shard_map/pallas_call | solution.py:348

commit v3 on v2

--- a/solution.py
+++ b/solution.py
@@ -12,11 +12,15 @@
 PLANE = 2 * NY * NX
 SEC, TERM, B, ROOTS = 6, 12, 256, 4
 CELLS = NZ * SEC * B * B
-NEAR = 4
-SOURCE = {1: 0, 2: 1, 3: 2, 4: 3, 5: 0, 6: 5, 7: 6, 8: 7}
+NEAR = 3
+SOURCE = {1: 0, 2: 1, 3: 2, 4: 0, 5: 4, 6: 4, 7: 6, 8: 6}
+FAR_FIRST = sorted(
+    ((dy, dx) for dy in range(NY) for dx in range(NX) if dy or dx),
+    key=lambda o: -min(o[0], NY - o[0]) - min(o[1], NX - o[1]),
+)
 EVENTS = (
-    "O0", "F0", "Z1", "P1", "Z5", "P5", "Z2", "P2", "C1", "Z6", "P6", "Z3", "P3", "C5", "Z7",
-    "P7", "C2", "C6", "Z8", "P8", "Z4", "P4", "C3", "C7", "Q0", "C8", "C4",
+    "O0", "F0", "Z1", "P1", "Z4", "P4", "Z2", "P2", "Z5", "P5", "C1", "Z6", "P6", "C4", "Z3",
+    "P3", "Z7", "P7", "C2", "Z8", "P8", "C5", "C6", "Q0", "C3", "C7", "C8",
 )
 
 
@@ -249,8 +253,8 @@
         total = part[u] + d2d_r[u].astype(F32)
         part[u] = total
         rs_s[u] = total.astype(BF)
-        for i in range(1, 16):
-            ch = (chip + i) % 16
+        for dy, dx in FAR_FIRST:
+            ch = (y + dy) % NY * NX + (x + dx) % NX
             remote(rs_s.at[u, ch], rs_r.at[u, chip], r_send.at[u], r_recv.at[u], (ch * 2 + c, z)).start()
 
     for u in range(3):

time: 59.1 us -> 59.3 us (level)
  no operation moved by 1% of the time
where the time goes in v3:
time: 59.3 us; the launch traced here: 59.1 us
  Pallas kernels  58.5 us (99%)
  between operations  0.64 us (1%)
    pallas_call x1, Pallas kernels, per_device(): pl.pallas_call(kernel, out_shape=(jax.ShapeDtypeStruct((3, 16, B), F32),...  56.8 us
    pallas_call x1, Pallas kernels, per_device(): pl.pallas_call(finish, out_shape=(jax.ShapeDtypeStruct((SEC, 8, B), F32),...  1.66 us

profile of v3, /device:TPU:1, one launch (start us, length us, event | category | flops | bytes accessed | tf_op | source)
XLA Modules:
  0.0 59.1 jit_solution(17704781163464643049)
XLA Ops:
  0.6 56.8 %shard_map.86 = (f32[3,16,256]{2,1,0:T(8,128)}, f32[8,128]{1,0:T(8,128)}) custom-call(bf16[6,256,256]{2,1,0:T(8,128)(2,1)} %psi_hbm.1, s32[1,16]{1,0:T(1,128)} %bitcast.5, s32[1,16]{1,0:T(1,128)} %bitcast.6, s32[6,12]{1,0:T(8,128)} %bitcast.4, bf16[3072,256]{1,0:T(8,128)(2,1)} %bitcast.3, bf16[12,256,256]{2,1,0:T(8,128)(2,1)} %rb_hbm.1, ...), custom_call_target="tpu_custom_call" | custom-call | tf_op jit(solution)/shard_map/pallas_call | solution.py:339
  57.5 1.7 %shard_map.87 = (f32[6,8,256]{2,1,0:T(8,128)}, f32[4]{0:T(128)}) custom-call(f32[3,16,256]{2,1,0:T(8,128)} %get-tuple-element.4.part, f32[8,128]{1,0:T(8,128)} %get-tuple-element.5.corr_rows, f32[4]{0:T(128)} %shift.1, bf16[4,6,8,256]{3,2,1,0:T(8,128)(2,1)} %roots.1), custom_call_target="tpu_custom_call" | custom-call | tf_op jit(solution)/shard_map/pallas_call | solution.py:352
